TPU v7x, 256 devices: a whole 4x4x8 slice. The times are simulated.
256 devices in a mesh: pb: 32 (over y, x, core), ka: 8 (over z).
Axes of the slice: x: 4, y: 4, z: 8, core: 2. Of those that a mesh axis runs over, the one named last changes fastest.
Arguments:
- queries: bfloat16 [16384, 1024], P('pb'), may hold values from -8 to 8
- keys: bfloat16 [8, 2048, 128], P('ka', 'pb'), may hold values from -4 to 4
- values: bfloat16 [8, 2048, 128], P('ka', 'pb'), may hold values from -4 to 4
- span_of: int32 [64], replicated, may hold values from 0 to 63, as said below
Outputs:
- attended: bfloat16 [16384, 1024], P('pb', 'ka')
- log_norm: float32 [8, 16384], P('ka', 'pb')
Inputs may be any that keep to these rules, and one draw needn't show every extreme that they name: `span_of`: for each index p of pb, slots 2 p and 2 p + 1 hold a span c and its mirror 64 - 1 - c, in either order; every span is held once.
All inputs are finite; a program needn't handle non-finite values.
Results may differ from a plain program's by a relative error of at most 0.018.
Values may be sent and summed in bfloat16 or wider, within the bound.
No kernel may reach another device: no remote copies, remote signals or barrier semaphores. Data moves between devices by JAX's collectives and lax.ppermute only.
A program may use at most 128 MiB of HBM per device.

v0:
```python
import math
import jax
import jax.numpy as jnp
from jax import lax
from jax.sharding import PartitionSpec as P

NEG = -1e30


def lookup(table, index):
    match = index[:, None] == jnp.arange(table.shape[0], dtype=jnp.int32)[None, :]
    return jnp.sum(jnp.where(match, table[None, :], 0), axis=1)


def update(state, block_keys, block_values, block_pos, query_flat, pos_flat, scale):
    best, total, accum = state
    scores = (
        lax.dot_general(
            query_flat, block_keys, (((1,), (1,)), ((), ())), preferred_element_type=jnp.float32
        )
        * scale
    )
    seen = block_pos[None, :] <= pos_flat[:, None]
    newbest = jnp.maximum(best, jnp.max(jnp.where(seen, scores, NEG), axis=1))
    factor = jnp.exp(best - newbest)
    weights = jnp.where(seen, jnp.exp(scores - newbest[:, None]), 0.0)
    total = total * factor + jnp.sum(weights, axis=1)
    accum = accum * factor[:, None] + jnp.dot(
        weights.astype(jnp.bfloat16), block_values, preferred_element_type=jnp.float32
    )
    return (newbest, total, accum)


def local(queries, keys, values, span_of):
    group = lax.axis_index("ka")
    groups = lax.axis_size("ka")
    place = lax.axis_index("pb")
    rows, width = queries.shape
    head_dim = keys.shape[2]
    heads = width // head_dim
    per_span = rows // 2
    key_rows = per_span // groups
    scale = 1.0 / math.sqrt(head_dim)
    local_spans = lookup(span_of, 2 * place + jnp.arange(2, dtype=jnp.int32))
    query_pos = (
        local_spans[:, None] * per_span + jnp.arange(per_span, dtype=jnp.int32)[None, :]
    ).reshape(rows)
    flat_queries = queries.reshape(rows * heads, head_dim)
    flat_pos = jnp.repeat(query_pos, heads)
    count = rows * heads
    state = (
        jnp.full((count,), NEG, jnp.float32),
        jnp.zeros((count,), jnp.float32),
        jnp.zeros((count, head_dim), jnp.float32),
    )
    start = jnp.int32(0)
    piece_keys = lax.all_gather(keys, "pb", axis=1, tiled=True)[0]
    piece_values = lax.all_gather(values, "pb", axis=1, tiled=True)[0]
    absorb_count = piece_keys.shape[0]
    step = min(absorb_count, 512)
    for first in range(0, absorb_count, step):
        size = min(step, absorb_count - first)
        index = start + first + jnp.arange(size, dtype=jnp.int32)
        block_pos = (
            lookup(span_of, index // key_rows) * per_span + index % key_rows * groups + group
        )
        state = update(
            state,
            piece_keys[first : first + size],
            piece_values[first : first + size],
            block_pos,
            flat_queries,
            flat_pos,
            scale,
        )
    best, total, accum = state
    partial_value = (
        (accum / jnp.maximum(total, 1.0)[:, None]).astype(jnp.bfloat16).reshape(rows, width)
    )
    best = best.reshape(rows, heads)
    total = total.reshape(rows, heads)
    local_heads = heads // groups
    received = lax.all_to_all(
        partial_value.reshape(1, rows, width), "ka", split_axis=2, concat_axis=0, tiled=True
    )
    got_best, got_total = (
        lax.all_to_all(best.reshape(1, rows, heads), "ka", split_axis=2, concat_axis=0, tiled=True),
        lax.all_to_all(
            total.reshape(1, rows, heads), "ka", split_axis=2, concat_axis=0, tiled=True
        ),
    )
    top = jnp.max(got_best, axis=0)
    share = got_total * jnp.exp(got_best - top)
    norm = jnp.sum(share, axis=0)
    pieces = received.reshape(groups, rows, local_heads, head_dim).astype(jnp.float32)
    merged = jnp.sum(share[..., None] * pieces, axis=0) / norm[..., None]
    attended = merged.reshape(rows, local_heads * head_dim).astype(jnp.bfloat16)
    log_norm = (top + jnp.log(norm)).T
    return (attended, log_norm)


def solution(mesh):
    placed = (P("pb", None), P("ka", "pb", None), P("ka", "pb", None), P())
    return jax.shard_map(
        local, mesh=mesh, in_specs=placed, out_specs=(P("pb", "ka"), P("ka", "pb")), check_vma=False
    )
```

profile of v0, /device:TPU:1, one launch (start us, length us, event | category | flops | bytes accessed | tf_op | source)
XLA Modules:
  0.0 185.1 jit_solution(387766933692637548)
XLA Ops:
  0.7 1.5 reshape.520
  2.2 26.4 %all_gather.6 = bf16[1,2048,128]{2,1,0:T(8,128)(2,1)S(1)} all-gather(bf16[1,64,128]{2,1,0:T(8,128)(2,1)} %param.5), channel_id=1, replica_groups=mesh['pb'=32,'ka'=8] {'pb'}, dimensions={1}, use_global_device_ids=true | all-gather | bytes 540672 | tf_op jit(solution)/shard_map/all_gather | solution.py:57
  28.6 4.5 %fusion.38 = f32[4096,512]{0,1:T(8,128)} fusion(bf16[4096,128]{1,0:T(8,128)(2,1)S(1)} %reshape.520, bf16[1,2048,128]{2,1,0:T(8,128)(2,1)S(1)} %all_gather.6), kind=kOutput, calls=%fused_computation.53 | convolution fusion | flops 536870912 | bytes 9568256 | tf_op jit(solution)/shard_map/dot_general | solution.py:18
  33.1 4.5 %fusion.39 = f32[4096,512]{0,1:T(8,128)} fusion(bf16[4096,128]{1,0:T(8,128)(2,1)S(1)} %reshape.520, bf16[1,2048,128]{2,1,0:T(8,128)(2,1)S(1)} %all_gather.6), kind=kOutput, calls=%fused_computation.55 | convolution fusion | flops 536870912 | bytes 9568256 | tf_op jit(solution)/shard_map/dot_general | solution.py:18
  37.6 0.2 fusion.75
  37.9 0.1 broadcast_in_dim.101
  38.0 0.2 le.21
  38.1 0.2 select_reduce_fusion
  38.3 4.5 %fusion = (f32[4096]{0:T(1024)S(1)}, f32[4096,512]{0,1:T(8,128)}) fusion(s32[4096]{0:T(1024)S(1)} %le.21, s32[512]{0:T(512)S(1)} %get-tuple-element.37, bf16[4096,128]{1,0:T(8,128)(2,1)S(1)} %reshape.520, bf16[1,2048,128]{2,1,0:T(8,128)(2,1)S(1)} %all_gather.6), kind=kOutput, calls=%fused_computation.8 | convolution fusion | flops 545255424 | bytes 9603072 | tf_op jit(solution)/shard_map/dot_general | solution.py:18
  42.9 0.2 max_broadcast_in_dim.46
  43.0 16.2 %fusion.5 = (f32[4096]{0:T(1024)S(1)}, f32[4096]{0:T(1024)S(1)}, f32[4096]{0:T(1024)S(1)}, f32[4096]{0:T(1024)S(1)}, f32[4096,512]{0,1:T(8,128)}) fusion(f32[4096,512]{0,1:T(8,128)} %get-tuple-element.32, f32[4096]{0:T(1024)S(1)} %broadcast_maximum_fusion, s32[4096]{0:T(1024)S(1)} %le.21, s32[512]{0:T(512)S(1)} %get-tuple-element.37, ...), kind=kOutput, calls=%fused_computation.13 | convolution fusion | flops 572506112 | bytes 34840576 | tf_op jit(solution)/shard_map/dot_general | solution.py:18
  59.3 0.2 reduce_max.53
  59.4 0.2 reduce_max.55
  59.6 0.2 reduce_max.57
  59.8 0.1 copy.20
  59.9 0.1 copy.23
  60.0 0.1 copy.17
  60.1 11.3 %fusion.7 = (f32[4096]{0:T(1024)S(1)}, f32[4096]{0:T(1024)S(1)}, f32[4096]{0:T(1024)S(1)}) fusion(f32[4096,512]{0,1:T(8,128)} %get-tuple-element.33, f32[4096]{0:T(1024)S(1)} %get-tuple-element.29, s32[4096]{0:T(1024)S(1)} %le.21, s32[512]{0:T(512)S(1)} %get-tuple-element.34, f32[4096]{0:T(1024)S(1)} %get-tuple-element.27, f32[4096,512]{0,1:T(8,128)} %fusion.38, ...), kind=kLoop, calls=%fused_computation.15 | loop fusion | flops 31444992 | bytes 25286656 | tf_op jit(solution)/shard_map/reduce_sum | solution.py:27
  71.4 0.2 reduce_sum.113
  71.6 0.1 copy.22
  71.6 0.2 reduce_sum.116
  71.8 0.1 copy.24
  71.9 0.2 reduce_sum.119
  72.1 0.1 copy.26
  72.2 0.2 reduce_sum.110
  72.4 0.1 copy.18
  72.5 0.1 copy.25
  72.6 0.6 copy.28
  73.2 8.2 %all-to-all-start.1 = ((f32[1,512,8]{1,0,2:T(1,128)}), f32[1,512,8]{1,0,2:T(1,128)S(1)}, u32[]{:S(2)}, u32[]{:S(2)}) async-start(f32[1,512,8]{1,0,2:T(1,128)} %copy.28), calls=%async_computation.1 | async-start | bytes 32768 | tf_op jit(solution)/shard_map/all_to_all | solution.py:87
  81.5 24.7 %all_gather.7 = bf16[1,2048,128]{2,1,0:T(8,128)(2,1)S(1)} all-gather(bf16[1,64,128]{2,1,0:T(8,128)(2,1)S(1)} %copy-done), channel_id=1, replica_groups=mesh['pb'=32,'ka'=8] {'pb'}, dimensions={1}, use_global_device_ids=true | all-gather | bytes 540672 | tf_op jit(solution)/shard_map/all_gather | solution.py:58
  106.2 5.6 %fusion.14 = f32[4096,128]{1,0:T(8,128)S(1)} fusion(f32[4096,512]{0,1:T(8,128)} %get-tuple-element.32, f32[4096]{0:T(1024)S(1)} %broadcast_maximum_fusion, s32[4096]{0:T(1024)S(1)} %le.21, s32[512]{0:T(512)S(1)} %get-tuple-element.37, f32[4096]{0:T(1024)S(1)} %get-tuple-element.26, f32[4096]{0:T(1024)S(1)} %get-tuple-element.30, ...), kind=kOutput, calls=%fused_computation.26 | convolution fusion | flops 548405248 | bytes 10684416 | tf_op jit(solution)/shard_map/dot_general | solution.py:28
  111.8 2.5 %fusion.13 = f32[4096,128]{1,0:T(8,128)S(1)} fusion(f32[4096,128]{1,0:T(8,128)S(1)} %fusion.14, f32[4096,512]{0,1:T(8,128)S(1)} %bitcast.78, f32[4096]{0:T(1024)S(1)} %get-tuple-element.29, s32[4096]{0:T(1024)S(1)} %le.21, s32[512]{0:T(512)S(1)} %get-tuple-element.34, f32[4096]{0:T(1024)S(1)} %get-tuple-element.25, bf16[1,2048,128]{2,1,0:T(8,128)(2,1)S(1)} %all_gather.7), kind=kOutput, calls=%fused_computation.24 | convolution fusion | flops 548405248 | bytes 12765184 | tf_op jit(solution)/shard_map/dot_general | solution.py:28
  114.3 0.9 slice-done.1
  115.3 3.9 %fusion.12 = f32[4096,128]{1,0:T(8,128)} fusion(f32[4096,128]{1,0:T(8,128)S(1)} %fusion.13, f32[4096,512]{0,1:T(8,128)S(1)} %bitcast.75, f32[4096]{0:T(1024)S(1)} %get-tuple-element.28, s32[4096]{0:T(1024)S(1)} %le.21, s32[512]{0:T(512)S(1)} %get-tuple-element.35, f32[4096]{0:T(1024)S(1)} %get-tuple-element.24, bf16[1,2048,128]{2,1,0:T(8,128)(2,1)S(1)} %all_gather.7), kind=kOutput, calls=%fused_computation.22 | convolution fusion | flops 548405248 | bytes 12765184 | tf_op jit(solution)/shard_map/dot_general | solution.py:28
  119.1 0.6 copy.27
  119.8 6.9 %all-to-all-start = ((f32[1,512,8]{1,0,2:T(1,128)}), f32[1,512,8]{1,0,2:T(1,128)S(1)}, u32[]{:S(2)}, u32[]{:S(2)}) async-start(f32[1,512,8]{1,0,2:T(1,128)} %copy.27), calls=%async_computation | async-start | bytes 32768 | tf_op jit(solution)/shard_map/all_to_all | solution.py:88
  126.7 6.5 %fusion.16 = bf16[4096,128]{1,0:T(8,128)(2,1)S(1)} fusion(f32[4096,128]{1,0:T(8,128)} %fusion.12, f32[4096,512]{0,1:T(8,128)} %fusion.38, f32[4096]{0:T(1024)S(1)} %get-tuple-element.27, s32[4096]{0:T(1024)S(1)} %le.21, s32[512]{0:T(512)S(1)} %get-tuple-element.36, f32[4096]{0:T(1024)S(1)} %get-tuple-element.23, bf16[1,2048,128]{2,1,0:T(8,128)(2,1)S(1)} %all_gather.7), kind=kOutput, calls=%fused_computation.28 | convolution fusion | flops 548929536 | bytes 11716608 | tf_op jit(solution)/shard_map/dot_general | solution.py:28
  133.2 0.5 reshape_reshape.2
  133.7 1.8 copy.29
  135.5 0.5 broadcast.448
  136.0 7.0 %reduce.6 = bf16[1024,512]{1,0:T(8,128)(2,1)S(1)} reduce(bf16[1024,1,512]{2,1,0:T(2,128)(2,1)S(1)} %bitcast.79, bf16[]{:T(256)} %broadcast.448), dimensions={1}, to_apply=%bitcast.64.reduce_sub_computation | reduce | bytes 2097154
  143.1 1.6 reshape.523
  144.7 6.6 %all-to-all-start.2 = ((bf16[8,2,32768]{2,1,0:T(2,128)(2,1)}), bf16[8,2,32768]{2,1,0:T(2,128)(2,1)S(1)}, u32[]{:S(2)}, u32[]{:S(2)}) async-start(bf16[8,2,32768]{2,1,0:T(2,128)(2,1)} %reshape.523), calls=%async_computation.2 | async-start | bytes 2097152 | tf_op jit(solution)/shard_map/all_to_all | solution.py:83
  151.4 0.6 log_add_fusion
  152.0 28.6 %all-to-all-done.2 = bf16[8,2,32768]{2,1,0:T(2,128)(2,1)S(1)} async-done(((bf16[8,2,32768]{2,1,0:T(2,128)(2,1)}), bf16[8,2,32768]{2,1,0:T(2,128)(2,1)S(1)}, u32[]{:S(2)}, u32[]{:S(2)}) %all-to-all-start.2) | async-done | bytes 1048608 | tf_op jit(solution)/shard_map/all_to_all | solution.py:83
  180.6 1.0 reshape.524
  181.6 2.7 %fusion.37 = f32[512,128]{0,1:T(8,128)S(1)} fusion(bf16[1,512,8,128]{1,0,3,2:T(2,128)(2,1)S(1)} %bitcast.76, f32[8,512]{1,0:T(8,128)S(1)} %fusion.43), kind=kLoop, calls=%fused_computation.46 | loop fusion | flops 1507328 | bytes 1327104 | tf_op jit(solution)/shard_map/reduce_sum | solution.py:96
  184.3 0.8 copy.30
  (34 shorter events, 0.4 us)
Async XLA Ops:
  33.1 4.5 %copy-start.1 = (s32[64]{0:T(128)S(1)}, s32[64]{0:T(128)}, u32[]{:S(2)}) copy-start(s32[64]{0:T(128)} %param.7) | copy-start | bytes 772
  60.1 21.4 %copy-start = (bf16[1,64,128]{2,1,0:T(8,128)(2,1)S(1)}, bf16[1,64,128]{2,1,0:T(8,128)(2,1)}, u32[]{:S(2)}) copy-start(bf16[1,64,128]{2,1,0:T(8,128)(2,1)} %param.6) | copy-start | bytes 49156
  73.2 46.5 %all-to-all-start.1 = ((f32[1,512,8]{1,0,2:T(1,128)}), f32[1,512,8]{1,0,2:T(1,128)S(1)}, u32[]{:S(2)}, u32[]{:S(2)}) async-start(f32[1,512,8]{1,0,2:T(1,128)} %copy.28), calls=%async_computation.1 | async-start | bytes 32768 | tf_op jit(solution)/shard_map/all_to_all | solution.py:87
  81.4 30.4 %slice-start.2 = ((s8[8388608]{0:T(1024)(128)(4,1)}), s8[4194304]{0:T(1024)(128)(4,1)S(1)}, s32[]{:S(2)}) async-start(s8[8388608]{0:T(1024)(128)(4,1)} %bitcast.77), calls=%async_computation.5 | async-start | bytes 8388608
  106.2 5.7 %slice-start.3 = ((s8[8388608]{0:T(1024)(128)(4,1)}), s8[4194304]{0:T(1024)(128)(4,1)S(1)}, s32[]{:S(2)}) async-start(s8[8388608]{0:T(1024)(128)(4,1)} %bitcast.77), calls=%async_computation.6 | async-start | bytes 8388608
  111.8 2.5 %slice-start = ((s8[8388608]{0:T(1024)(128)(4,1)}), s8[4194304]{0:T(1024)(128)(4,1)S(1)}, s32[]{:S(2)}) async-start(s8[8388608]{0:T(1024)(128)(4,1)} %bitcast.74), calls=%async_computation.3 | async-start | bytes 8388608
  111.8 3.4 %slice-start.1 = ((s8[8388608]{0:T(1024)(128)(4,1)}), s8[4194304]{0:T(1024)(128)(4,1)S(1)}, s32[]{:S(2)}) async-start(s8[8388608]{0:T(1024)(128)(4,1)} %bitcast.74), calls=%async_computation.4 | async-start | bytes 8388608
  119.8 24.9 %all-to-all-start = ((f32[1,512,8]{1,0,2:T(1,128)}), f32[1,512,8]{1,0,2:T(1,128)S(1)}, u32[]{:S(2)}, u32[]{:S(2)}) async-start(f32[1,512,8]{1,0,2:T(1,128)} %copy.27), calls=%async_computation | async-start | bytes 32768 | tf_op jit(solution)/shard_map/all_to_all | solution.py:88
  144.7 35.9 %all-to-all-start.2 = ((bf16[8,2,32768]{2,1,0:T(2,128)(2,1)}), bf16[8,2,32768]{2,1,0:T(2,128)(2,1)S(1)}, u32[]{:S(2)}, u32[]{:S(2)}) async-start(bf16[8,2,32768]{2,1,0:T(2,128)(2,1)} %reshape.523), calls=%async_computation.2 | async-start | bytes 2097152 | tf_op jit(solution)/shard_map/all_to_all | solution.py:83
where the time goes:
time: 185 us
  blocking collectives  51.1 us (28%)
  matrix products  48.1 us (26%)
  waiting for transfers between devices  28.6 us (15%)
  other arithmetic  22.3 us (12%)
  starting transfers between devices  21.8 us (12%)
  local copies, waits for them, and re-layouts  12.3 us (7%)
    dot_general x4, matrix products, update(): lax.dot_general(query_flat, block_keys, (((1,), (1,)), ((), ())), preferr...  29.7 us
    all_to_all x1, waiting for transfers between devices, local(): lax.all_to_all(partial_value.reshape(1, rows, width), 'ka', split_axis=2,...  28.6 us
    all_gather x1, blocking collectives, local(): piece_keys = lax.all_gather(keys, 'pb', axis=1, tiled=True)[0]  26.4 us
    all_gather x1, blocking collectives, local(): piece_values = lax.all_gather(values, 'pb', axis=1, tiled=True)[0]  24.7 us
    dot_general x4, matrix products, update(): jnp.dot(weights.astype(jnp.bfloat16), block_values, preferred_element_typ...  18.4 us
    reduce_sum x1, other arithmetic, update(): total = total * factor + jnp.sum(weights, axis=1)  11.3 us
    all_to_all x1, starting transfers between devices, local(): lax.all_to_all(best.reshape(1, rows, heads), 'ka', split_axis=2, concat_a...  8.19 us
    unnamed x4, other arithmetic  7.12 us
  transfers between devices with their start and end apart: 3, of which 1 were waited for; matrix products, arithmetic and copies ran while one was open for 17% of the time, Pallas kernels for 0%

commit v1 on v0

--- a/solution.py
+++ b/solution.py
@@ -54,7 +54,9 @@
         jnp.zeros((count, head_dim), jnp.float32),
     )
     start = jnp.int32(0)
-    piece_keys = lax.all_gather(keys, "pb", axis=1, tiled=True)[0]
+    piece_keys = jnp.concatenate(
+        lax.all_to_all(jnp.stack([keys] * lax.axis_size("pb")), "pb", 0, 0), axis=1
+    )[0]
     piece_values = lax.all_gather(values, "pb", axis=1, tiled=True)[0]
     absorb_count = piece_keys.shape[0]
     step = min(absorb_count, 512)

time: 185 us -> 175 us (0.946)
  blocking collectives: 51.1 us -> 27.1 us
  starting transfers between devices: 21.8 us -> 30.1 us
    all_gather x1 -> x0, blocking collectives: 26.4 us -> none  [local(): piece_keys = lax.all_gather(keys, 'pb', axis=1, tiled=True)[0]]
    all_to_all x0 -> x1, starting transfers between devices: none -> 8.59 us  [local(): lax.all_to_all(jnp.stack([keys] * lax.axis_size('pb')), 'pb', 0, 0)]
    all_gather x1, blocking collectives: 24.7 us -> 27.1 us  [local(): piece_values = lax.all_gather(values, 'pb', axis=1, tiled=True)[0]]
    dot_general x4, matrix products: 18.4 us -> 20.7 us  [update(): jnp.dot(weights.astype(jnp.bfloat16), block_values, preferred_element_typ...]
    unnamed x17 -> x9, local copies, waits for them, and re-layouts: 4.88 us -> 4.79 us
    unnamed x4 -> x3, other arithmetic: 7.12 us -> 7.12 us
  transfers between devices with their start and end apart: 3 -> 4, of which waited for: 1 -> 1; matrix products, arithmetic and copies ran while one was open for 17% -> 21% of each run, Pallas kernels for 0% -> 0%
where the time goes in v1:
time: 175 us; the launch traced here: 174 us
  matrix products  49.8 us (28%)
  starting transfers between devices  30.1 us (17%)
  waiting for transfers between devices  28.5 us (16%)
  blocking collectives  27.1 us (15%)
  other arithmetic  23.6 us (13%)
  local copies, waits for them, and re-layouts  14.1 us (8%)
    dot_general x4, matrix products, update(): lax.dot_general(query_flat, block_keys, (((1,), (1,)), ((), ())), preferr...  29.1 us
    all_to_all x1, waiting for transfers between devices, local(): lax.all_to_all(partial_value.reshape(1, rows, width), 'ka', split_axis=2,...  28.5 us
    all_gather x1, blocking collectives, local(): piece_values = lax.all_gather(values, 'pb', axis=1, tiled=True)[0]  27.1 us
    dot_general x4, matrix products, update(): jnp.dot(weights.astype(jnp.bfloat16), block_values, preferred_element_typ...  20.7 us
    reduce_sum x1, other arithmetic, update(): total = total * factor + jnp.sum(weights, axis=1)  11.3 us
    all_to_all x1, starting transfers between devices, local(): lax.all_to_all(jnp.stack([keys] * lax.axis_size('pb')), 'pb', 0, 0)  8.59 us
    all_to_all x1, starting transfers between devices, local(): lax.all_to_all(best.reshape(1, rows, heads), 'ka', split_axis=2, concat_a...  8.18 us
    unnamed x3, other arithmetic  7.12 us
  transfers between devices with their start and end apart: 4, of which 1 were waited for; matrix products, arithmetic and copies ran while one was open for 21% of the time, Pallas kernels for 0%

profile of v1, /device:TPU:1, one launch (start us, length us, event | category | flops | bytes accessed | tf_op | source)
XLA Modules:
  0.0 174.0 jit_solution(14863978352008307544)
XLA Ops:
  0.6 1.6 stack.2
  2.3 8.6 %all-to-all-start = ((bf16[32,1,64,128]{3,2,1,0:T(8,128)(2,1)}), bf16[32,1,64,128]{3,2,1,0:T(8,128)(2,1)S(1)}, u32[]{:S(2)}, u32[]{:S(2)}) async-start(bf16[32,1,64,128]{3,2,1,0:T(8,128)(2,1)} %stack.2), calls=%async_computation | async-start | bytes 1048576 | tf_op jit(solution)/shard_map/all_to_all | solution.py:58
  10.9 0.8 fusion.71
  11.8 27.1 %all_gather.3 = bf16[1,2048,128]{2,1,0:T(8,128)(2,1)S(1)} all-gather(bf16[1,64,128]{2,1,0:T(8,128)(2,1)} %param.6), channel_id=1, replica_groups=mesh['pb'=32,'ka'=8] {'pb'}, dimensions={1}, use_global_device_ids=true | all-gather | bytes 540672 | tf_op jit(solution)/shard_map/all_gather | solution.py:60
  38.9 0.8 select_reduce_fusion
  39.8 0.1 broadcast_in_dim.101
  39.9 0.2 le.21
  40.0 1.7 reshape.523
  41.8 4.5 %fusion = (f32[4096]{0:T(1024)S(1)}, f32[4096,512]{0,1:T(8,128)}) fusion(s32[4096]{0:T(1024)S(1)} %le.21, s32[512]{0:T(512)S(1)} %get-tuple-element.41, bf16[4096,128]{1,0:T(8,128)(2,1)S(1)} %reshape.523, bf16[512,128]{1,0:T(8,128)(2,1)S(1)} %bitcast.76), kind=kOutput, calls=%fused_computation.8 | convolution fusion | flops 545255424 | bytes 9603072 | tf_op jit(solution)/shard_map/dot_general | solution.py:18
  46.4 4.5 %fusion.85 = f32[4096,512]{0,1:T(8,128)} fusion(bf16[4096,128]{1,0:T(8,128)(2,1)S(1)} %reshape.523, bf16[512,128]{1,0:T(8,128)(2,1)S(1)} %bitcast.72), kind=kOutput, calls=%fused_computation.145 | convolution fusion | flops 536870912 | bytes 9568256 | tf_op jit(solution)/shard_map/dot_general | solution.py:18
  50.8 4.5 %fusion.86 = f32[4096,512]{0,1:T(8,128)} fusion(bf16[4096,128]{1,0:T(8,128)(2,1)S(1)} %reshape.523, bf16[512,128]{1,0:T(8,128)(2,1)S(1)} %bitcast.71), kind=kOutput, calls=%fused_computation.146 | convolution fusion | flops 536870912 | bytes 9568256 | tf_op jit(solution)/shard_map/dot_general | solution.py:18
  55.3 0.2 max_broadcast_in_dim.46
  55.5 15.6 %fusion.5 = (f32[4096]{0:T(1024)S(1)}, f32[4096]{0:T(1024)S(1)}, f32[4096]{0:T(1024)S(1)}, f32[4096]{0:T(1024)S(1)}, f32[4096,512]{0,1:T(8,128)}) fusion(f32[4096,512]{0,1:T(8,128)} %get-tuple-element.36, f32[4096]{0:T(1024)S(1)} %broadcast_maximum_fusion, s32[4096]{0:T(1024)S(1)} %le.21, s32[512]{0:T(512)S(1)} %get-tuple-element.41, ...), kind=kOutput, calls=%fused_computation.13 | convolution fusion | flops 572506112 | bytes 34840576 | tf_op jit(solution)/shard_map/dot_general | solution.py:18
  71.1 0.2 reduce_max.53
  71.3 0.2 reduce_max.55
  71.4 0.2 reduce_max.57
  71.6 11.3 %fusion.7 = (f32[4096]{0:T(1024)S(1)}, f32[4096]{0:T(1024)S(1)}, f32[4096]{0:T(1024)S(1)}) fusion(f32[4096,512]{0,1:T(8,128)} %get-tuple-element.37, f32[4096]{0:T(1024)S(1)} %get-tuple-element.29, s32[4096]{0:T(1024)S(1)} %le.21, s32[512]{0:T(512)S(1)} %get-tuple-element.38, f32[4096]{0:T(1024)S(1)} %get-tuple-element.27, f32[4096,512]{0,1:T(8,128)} %fusion.86, ...), kind=kLoop, calls=%fused_computation.15 | loop fusion | flops 31444992 | bytes 25286656 | tf_op jit(solution)/shard_map/reduce_sum | solution.py:27
  82.9 0.2 reduce_sum.113
  83.1 0.2 reduce_sum.116
  83.2 0.2 reduce_sum.119
  83.4 0.2 reduce_sum.110
  83.7 0.1 copy.23
  83.8 0.1 copy.17
  83.9 0.1 copy.22
  84.0 0.1 copy.24
  84.1 0.1 copy.26
  84.2 0.1 copy.18
  84.3 0.1 copy.25
  84.4 0.6 copy.28
  85.1 8.2 %all-to-all-start.2 = ((f32[1,512,8]{1,0,2:T(1,128)}), f32[1,512,8]{1,0,2:T(1,128)S(1)}, u32[]{:S(2)}, u32[]{:S(2)}) async-start(f32[1,512,8]{1,0,2:T(1,128)} %copy.28), calls=%async_computation.2 | async-start | bytes 32768 | tf_op jit(solution)/shard_map/all_to_all | solution.py:89
  93.3 5.3 %fusion.14 = f32[4096,128]{1,0:T(8,128)S(1)} fusion(f32[4096,512]{0,1:T(8,128)} %get-tuple-element.36, f32[4096]{0:T(1024)S(1)} %broadcast_maximum_fusion, s32[4096]{0:T(1024)S(1)} %le.21, s32[512]{0:T(512)S(1)} %get-tuple-element.41, f32[4096]{0:T(1024)S(1)} %get-tuple-element.26, f32[4096]{0:T(1024)S(1)} %get-tuple-element.34, ...), kind=kOutput, calls=%fused_computation.26 | convolution fusion | flops 548405248 | bytes 10684416 | tf_op jit(solution)/shard_map/dot_general | solution.py:28
  98.5 5.0 %fusion.13 = f32[4096,128]{1,0:T(8,128)S(1)} fusion(f32[4096,128]{1,0:T(8,128)S(1)} %fusion.14, f32[4096,512]{0,1:T(8,128)} %get-tuple-element.37, f32[4096]{0:T(1024)S(1)} %get-tuple-element.29, s32[4096]{0:T(1024)S(1)} %le.21, s32[512]{0:T(512)S(1)} %get-tuple-element.38, f32[4096]{0:T(1024)S(1)} %get-tuple-element.25, ...), kind=kOutput, calls=%fused_computation.24 | convolution fusion | flops 548405248 | bytes 12765184 | tf_op jit(solution)/shard_map/dot_general | solution.py:28
  103.6 0.9 slice-done.1
  104.4 4.0 %fusion.12 = f32[4096,128]{1,0:T(8,128)} fusion(f32[4096,128]{1,0:T(8,128)S(1)} %fusion.13, f32[4096,512]{0,1:T(8,128)S(1)} %bitcast.68, f32[4096]{0:T(1024)S(1)} %get-tuple-element.28, s32[4096]{0:T(1024)S(1)} %le.21, s32[512]{0:T(512)S(1)} %get-tuple-element.39, f32[4096]{0:T(1024)S(1)} %get-tuple-element.24, bf16[1,2048,128]{2,1,0:T(8,128)(2,1)S(1)} %all_gather.3), kind=kOutput, calls=%fused_computation.22 | convolution fusion | flops 548405248 | bytes 12765184 | tf_op jit(solution)/shard_map/dot_general | solution.py:28
  108.4 0.6 copy.27
  109.0 6.6 %all-to-all-start.1 = ((f32[1,512,8]{1,0,2:T(1,128)}), f32[1,512,8]{1,0,2:T(1,128)S(1)}, u32[]{:S(2)}, u32[]{:S(2)}) async-start(f32[1,512,8]{1,0,2:T(1,128)} %copy.27), calls=%async_computation.1 | async-start | bytes 32768 | tf_op jit(solution)/shard_map/all_to_all | solution.py:90
  115.7 6.5 %fusion.16 = bf16[4096,128]{1,0:T(8,128)(2,1)S(1)} fusion(f32[4096,128]{1,0:T(8,128)} %fusion.12, f32[4096,512]{0,1:T(8,128)} %fusion.86, f32[4096]{0:T(1024)S(1)} %get-tuple-element.27, s32[4096]{0:T(1024)S(1)} %le.21, s32[512]{0:T(512)S(1)} %get-tuple-element.40, f32[4096]{0:T(1024)S(1)} %get-tuple-element.23, bf16[1,2048,128]{2,1,0:T(8,128)(2,1)S(1)} %all_gather.3), kind=kOutput, calls=%fused_computation.28 | convolution fusion | flops 548929536 | bytes 11716608 | tf_op jit(solution)/shard_map/dot_general | solution.py:28
  122.2 0.5 reshape_reshape.2
  122.7 1.8 %copy.29 = bf16[1,512,1024]{1,0,2:T(2,128)(2,1)S(1)} copy(bf16[1,512,1024]{2,1,0:T(8,128)(2,1)S(1)} %reshape_reshape.2) | data formatting | bytes 2097152 | tf_op jit(solution)/shard_map/reshape;reshape | solution.py:86
  124.5 0.5 broadcast.451
  125.0 7.0 %reduce.6 = bf16[1024,512]{1,0:T(8,128)(2,1)S(1)} reduce(bf16[1024,1,512]{2,1,0:T(2,128)(2,1)S(1)} %bitcast.70, bf16[]{:T(256)} %broadcast.451), dimensions={1}, to_apply=%bitcast.57.reduce_sub_computation | reduce | bytes 2097154
  132.1 1.6 reshape.526
  133.7 6.7 %all-to-all-start.3 = ((bf16[8,2,32768]{2,1,0:T(2,128)(2,1)}), bf16[8,2,32768]{2,1,0:T(2,128)(2,1)S(1)}, u32[]{:S(2)}, u32[]{:S(2)}) async-start(bf16[8,2,32768]{2,1,0:T(2,128)(2,1)} %reshape.526), calls=%async_computation.3 | async-start | bytes 2097152 | tf_op jit(solution)/shard_map/all_to_all | solution.py:85
  140.4 0.6 log_add_fusion
  141.0 28.5 %all-to-all-done.3 = bf16[8,2,32768]{2,1,0:T(2,128)(2,1)S(1)} async-done(((bf16[8,2,32768]{2,1,0:T(2,128)(2,1)}), bf16[8,2,32768]{2,1,0:T(2,128)(2,1)S(1)}, u32[]{:S(2)}, u32[]{:S(2)}) %all-to-all-start.3) | async-done | bytes 1048608 | tf_op jit(solution)/shard_map/all_to_all | solution.py:85
  169.5 1.0 reshape.527
  170.6 2.7 %fusion.37 = f32[512,128]{0,1:T(8,128)S(1)} fusion(bf16[1,512,8,128]{1,0,3,2:T(2,128)(2,1)S(1)} %bitcast.69, f32[8,512]{1,0:T(8,128)S(1)} %fusion.39), kind=kLoop, calls=%fused_computation.46 | loop fusion | flops 1507328 | bytes 1327104 | tf_op jit(solution)/shard_map/reduce_sum | solution.py:98
  173.3 0.8 copy.30
  (28 shorter events, 0.5 us)
Async XLA Ops:
  2.3 39.5 %all-to-all-start = ((bf16[32,1,64,128]{3,2,1,0:T(8,128)(2,1)}), bf16[32,1,64,128]{3,2,1,0:T(8,128)(2,1)S(1)}, u32[]{:S(2)}, u32[]{:S(2)}) async-start(bf16[32,1,64,128]{3,2,1,0:T(8,128)(2,1)} %stack.2), calls=%async_computation | async-start | bytes 1048576 | tf_op jit(solution)/shard_map/all_to_all | solution.py:58
  85.1 24.0 %all-to-all-start.2 = ((f32[1,512,8]{1,0,2:T(1,128)}), f32[1,512,8]{1,0,2:T(1,128)S(1)}, u32[]{:S(2)}, u32[]{:S(2)}) async-start(f32[1,512,8]{1,0,2:T(1,128)} %copy.28), calls=%async_computation.2 | async-start | bytes 32768 | tf_op jit(solution)/shard_map/all_to_all | solution.py:89
  98.5 5.0 %slice-start = ((s8[8388608]{0:T(1024)(128)(4,1)}), s8[4194304]{0:T(1024)(128)(4,1)S(1)}, s32[]{:S(2)}) async-start(s8[8388608]{0:T(1024)(128)(4,1)} %bitcast.67), calls=%async_computation.4 | async-start | bytes 8388608
  98.5 5.9 %slice-start.1 = ((s8[8388608]{0:T(1024)(128)(4,1)}), s8[4194304]{0:T(1024)(128)(4,1)S(1)}, s32[]{:S(2)}) async-start(s8[8388608]{0:T(1024)(128)(4,1)} %bitcast.67), calls=%async_computation.5 | async-start | bytes 8388608
  109.0 24.6 %all-to-all-start.1 = ((f32[1,512,8]{1,0,2:T(1,128)}), f32[1,512,8]{1,0,2:T(1,128)S(1)}, u32[]{:S(2)}, u32[]{:S(2)}) async-start(f32[1,512,8]{1,0,2:T(1,128)} %copy.27), calls=%async_computation.1 | async-start | bytes 32768 | tf_op jit(solution)/shard_map/all_to_all | solution.py:90
  133.7 35.8 %all-to-all-start.3 = ((bf16[8,2,32768]{2,1,0:T(2,128)(2,1)}), bf16[8,2,32768]{2,1,0:T(2,128)(2,1)S(1)}, u32[]{:S(2)}, u32[]{:S(2)}) async-start(bf16[8,2,32768]{2,1,0:T(2,128)(2,1)} %reshape.526), calls=%async_computation.3 | async-start | bytes 2097152 | tf_op jit(solution)/shard_map/all_to_all | solution.py:85
